TPU v7x, 512 devices: a whole 4x8x8 slice. The times are simulated.
512 devices in a mesh: ctx: 128 (over y, z, core), tp: 4 (over x).
Axes of the slice: x: 4, y: 8, z: 8, core: 2. Of those that a mesh axis runs over, the one named last changes fastest.
Arguments:
- y_first: bfloat16 [16384, 2048], P('ctx', 'tp'), may hold values from -6 to 6
- x_second: bfloat16 [16384, 2048], P('ctx', 'tp'), may hold values from -6 to 6
- grad_first: bfloat16 [16384, 2048], P('ctx', 'tp'), may hold values from -6 to 6
- grad_second: bfloat16 [16384, 2048], P('ctx', 'tp'), may hold values from -6 to 6
- w_query: bfloat16 [2048, 2048], P('ctx', 'tp'), may hold values from -0.125 to 0.125
- w_key: bfloat16 [2048, 2048], P('ctx', 'tp'), may hold values from -0.125 to 0.125
- w_value: bfloat16 [2048, 2048], P('ctx', 'tp'), may hold values from -0.125 to 0.125
- w_out: bfloat16 [2048, 2048], P('tp', 'ctx'), may hold values from -0.125 to 0.125
- norm_gain: float32 [2048], P('tp'), may hold values from 0.1 to 1.9
Outputs:
- x_first: bfloat16 [16384, 2048], P('ctx', 'tp')
- grad_x_second: bfloat16 [16384, 2048], P('ctx', 'tp')
All inputs are finite; a program needn't handle non-finite values.
Results may differ from a plain program's by a relative error of at most 0.015.
Values may be sent and summed in bfloat16 or wider, within the bound.
A program may use at most 192 MiB of HBM per device.

v0:
```python
import jax
import jax.numpy as jnp
from jax import lax
from jax.sharding import PartitionSpec as P

HEAD = 128


eps_norm = 1e-06
highest = lax.Precision.HIGHEST


def prefix(shard, axis, join, neutral, backward):
    count = lax.axis_size(axis)
    place = lax.axis_index(axis)
    ahead = count - 1 - place if backward else place
    gathered = lax.all_gather(shard.astype(jnp.bfloat16), axis)
    state = jnp.zeros_like(shard) + jnp.asarray(neutral, shard.dtype)

    def one(turn, state):
        source = count - 1 - turn if backward else turn
        return join(state, lax.dynamic_index_in_dim(gathered, source, 0, False).astype(shard.dtype))

    return lax.fori_loop(0, ahead, one, state)


def feature_map(pre):
    return jnp.where(pre > 0, pre + 1.0, jnp.exp(jnp.minimum(pre, 0.0)))


def feature_slope(pre):
    return jnp.where(pre > 0, 1.0, jnp.exp(jnp.minimum(pre, 0.0)))


def add_states(earlier, later):
    return earlier + later


def per_device(
    y_first, x_second, grad_first, grad_second, w_query, w_key, w_value, w_out, norm_gain
):
    tok_rows = x_second.shape[0]
    x_full = lax.all_gather(x_second, "tp", axis=1, tiled=True)
    query_full = lax.all_gather(w_query, "ctx", axis=0, tiled=True)
    key_full = lax.all_gather(w_key, "ctx", axis=0, tiled=True)
    value_full = lax.all_gather(w_value, "ctx", axis=0, tiled=True)
    out_full = lax.all_gather(w_out, "ctx", axis=1, tiled=True)
    pre_query = jnp.dot(x_full, query_full, preferred_element_type=jnp.float32)
    pre_key = jnp.dot(x_full, key_full, preferred_element_type=jnp.float32)
    query = feature_map(pre_query).astype(jnp.bfloat16)
    key_feat = feature_map(pre_key).astype(jnp.bfloat16)
    value = jnp.dot(x_full, value_full, preferred_element_type=jnp.float32).astype(jnp.bfloat16)
    head_count = query.shape[1] // HEAD
    query_heads = query.reshape(tok_rows, head_count, HEAD)
    key_heads = key_feat.reshape(tok_rows, head_count, HEAD)
    value_heads = value.reshape(tok_rows, head_count, HEAD)
    causal = jnp.arange(tok_rows)[:, None] >= jnp.arange(tok_rows)[None, :]
    empty_state = jnp.zeros((head_count, HEAD, HEAD), jnp.float32)
    local_state = jnp.einsum(
        "lhe,lhf->hef", key_heads, value_heads, preferred_element_type=jnp.float32
    )
    prior_state = prefix(local_state, "ctx", add_states, empty_state, False)
    scores = jnp.einsum("lhe,mhe->hlm", query_heads, key_heads, preferred_element_type=jnp.float32)
    attn_scores = jnp.where(causal[None], scores, 0.0).astype(jnp.bfloat16)
    inner = jnp.einsum("hlm,mhe->lhe", attn_scores, value_heads, preferred_element_type=jnp.float32)
    cross = jnp.einsum(
        "lhe,hef->lhf", query_heads.astype(jnp.float32), prior_state, precision=highest
    )
    attn_out = inner + cross
    rms_scale = jnp.sqrt(jnp.mean(attn_out * attn_out, axis=-1, keepdims=True) + eps_norm)
    unit_out = attn_out / rms_scale
    gain_heads = norm_gain.reshape(head_count, HEAD)
    normed = (unit_out * gain_heads).astype(jnp.bfloat16).reshape(tok_rows, head_count * HEAD)
    partial_out = jnp.dot(normed, out_full, preferred_element_type=jnp.float32)
    mixed_out = lax.psum_scatter(
        partial_out.astype(jnp.bfloat16), "tp", scatter_dimension=1, tiled=True
    ).astype(jnp.float32)
    x_first = (y_first.astype(jnp.float32) - mixed_out).astype(jnp.bfloat16)
    grad_full = lax.all_gather(grad_first, "tp", axis=1, tiled=True)
    grad_normed = jnp.einsum("td,fd->tf", grad_full, out_full, preferred_element_type=jnp.float32)
    scaled_grad = grad_normed.reshape(tok_rows, head_count, HEAD) * gain_heads
    grad_out = (
        (scaled_grad - unit_out * jnp.mean(unit_out * scaled_grad, axis=-1, keepdims=True))
        / rms_scale
    ).astype(jnp.bfloat16)
    local_back = jnp.einsum(
        "lhe,lhf->hef", query_heads, grad_out, preferred_element_type=jnp.float32
    )
    later_state = prefix(local_back, "ctx", add_states, empty_state, True)
    back_scores = jnp.einsum(
        "lhf,mhf->hlm", grad_out, value_heads, preferred_element_type=jnp.float32
    )
    grad_scores = jnp.where(causal[None], back_scores, 0.0).astype(jnp.bfloat16)
    grad_query = jnp.einsum(
        "hlm,mhe->lhe", grad_scores, key_heads, preferred_element_type=jnp.float32
    )
    grad_query = grad_query + jnp.einsum(
        "lhf,hef->lhe", grad_out.astype(jnp.float32), prior_state, precision=highest
    )
    grad_key = jnp.einsum(
        "hlm,lhe->mhe", grad_scores, query_heads, preferred_element_type=jnp.float32
    )
    grad_key = grad_key + jnp.einsum(
        "mhf,hef->mhe", value_heads.astype(jnp.float32), later_state, precision=highest
    )
    grad_value = jnp.einsum(
        "hlm,lhf->mhf", attn_scores, grad_out, preferred_element_type=jnp.float32
    )
    grad_value = grad_value + jnp.einsum(
        "mhe,hef->mhf", key_heads.astype(jnp.float32), later_state, precision=highest
    )
    feature_cols = head_count * HEAD
    query_pre_grad = (grad_query.reshape(tok_rows, feature_cols) * feature_slope(pre_query)).astype(
        jnp.bfloat16
    )
    key_pre_grad = (grad_key.reshape(tok_rows, feature_cols) * feature_slope(pre_key)).astype(
        jnp.bfloat16
    )
    value_pre_grad = grad_value.reshape(tok_rows, feature_cols).astype(jnp.bfloat16)
    terms = jnp.einsum("tf,df->td", query_pre_grad, query_full, preferred_element_type=jnp.float32)
    terms = terms + jnp.einsum(
        "tf,df->td", key_pre_grad, key_full, preferred_element_type=jnp.float32
    )
    terms = terms + jnp.einsum(
        "tf,df->td", value_pre_grad, value_full, preferred_element_type=jnp.float32
    )
    summed = lax.psum_scatter(
        terms.astype(jnp.bfloat16), "tp", scatter_dimension=1, tiled=True
    ).astype(jnp.float32)
    grad_x_second = (grad_second.astype(jnp.float32) + summed).astype(jnp.bfloat16)
    return (x_first, grad_x_second)


def solution(mesh):
    in_specs = (
        P("ctx", "tp"),
        P("ctx", "tp"),
        P("ctx", "tp"),
        P("ctx", "tp"),
        P("ctx", "tp"),
        P("ctx", "tp"),
        P("ctx", "tp"),
        P("tp", "ctx"),
        P("tp"),
    )
    out_specs = (P("ctx", "tp"), P("ctx", "tp"))
    return jax.shard_map(
        per_device, mesh=mesh, in_specs=in_specs, out_specs=out_specs, check_vma=False
    )
```

profile of v0, /device:TPU:1, one launch (start us, length us, event | category | flops | bytes accessed | tf_op | source)
XLA Modules:
  0.0 749.2 jit_solution(10619423629113050844)
XLA Ops:
  9.4 11.3 %all_gather.30 = bf16[128,2048]{1,0:T(8,128)(2,1)S(1)} all-gather(bf16[128,512]{1,0:T(8,128)(2,1)} %param.14), channel_id=1, replica_groups=mesh['ctx'=128,'tp'=4] {'tp'}, dimensions={1}, use_global_device_ids=true | all-gather | bytes 655360 | tf_op jit(solution)/shard_map/all_gather | solution.py:43
  20.7 79.2 %all-gather.13.cloned.1.call-done = bf16[2048,512]{1,0:T(8,128)(2,1)} async-done(((bf16[16,512]{1,0:T(8,128)(2,1)}), bf16[2048,512]{1,0:T(8,128)(2,1)}) %all-gather.13.cloned.1.call-update) | async-done | bytes 2097168 | tf_op jit(solution)/shard_map/all_gather | solution.py:45
  99.9 2.8 select_convert_fusion
  102.8 80.1 %all-gather.9.cloned.1.call-done = bf16[2048,512]{1,0:T(8,128)(2,1)} async-done(((bf16[16,512]{1,0:T(8,128)(2,1)}), bf16[2048,512]{1,0:T(8,128)(2,1)}) %all-gather.9.cloned.1.call-update) | async-done | bytes 2097168 | tf_op jit(solution)/shard_map/all_gather | solution.py:46
  182.9 2.0 fusion.5
  186.5 11.0 %all_gather.37 = bf16[128,2048]{1,0:T(8,128)(2,1)S(1)} all-gather(bf16[128,512]{1,0:T(8,128)(2,1)S(1)} %copy-done.5), channel_id=1, replica_groups=mesh['ctx'=128,'tp'=4] {'tp'}, dimensions={1}, use_global_device_ids=true | all-gather | bytes 655360 | tf_op jit(solution)/shard_map/all_gather | solution.py:79
  197.4 68.4 %all-gather.11.cloned.1.call-done = bf16[2048,512]{1,0:T(8,128)(2,1)} async-done(((bf16[16,512]{1,0:T(8,128)(2,1)}), bf16[2048,512]{1,0:T(8,128)(2,1)}) %all-gather.11.cloned.1.call-update) | async-done | bytes 2097168 | tf_op jit(solution)/shard_map/all_gather | solution.py:44
  265.9 2.8 select_convert_fusion.1
  269.2 97.7 %all-gather.17.cloned.1.call-done = bf16[512,128,128]{2,1,0:T(8,128)(2,1)} async-done(((bf16[4,128,128]{2,1,0:T(8,128)(2,1)}), bf16[512,128,128]{2,1,0:T(8,128)(2,1)}) %all-gather.17.cloned.1.call-update) | async-done | bytes 16777232 | tf_op jit(solution)/shard_map/all_gather | solution.py:17
  368.3 82.4 %all-gather.15.cloned.1.call-done = bf16[512,2048]{0,1:T(8,128)(2,1)} async-done(((bf16[512,16]{0,1:T(8,128)(2,1)}), bf16[512,2048]{0,1:T(8,128)(2,1)}) %all-gather.15.cloned.1.call-update) | async-done | bytes 2097168 | tf_op jit(solution)/shard_map/all_gather | solution.py:47
  450.8 2.6 multiply_reduce_fusion
  457.8 3.3 convolution_convert_fusion
  461.2 1.7 fusion.6
  463.0 127.7 %all-gather.19.cloned.1.call-done = bf16[512,128,128]{2,1,0:T(8,128)(2,1)} async-done(((bf16[4,128,128]{2,1,0:T(8,128)(2,1)}), bf16[512,128,128]{2,1,0:T(8,128)(2,1)}) %all-gather.19.cloned.1.call-update) | async-done | bytes 16777232 | tf_op jit(solution)/shard_map/all_gather | solution.py:17
  590.7 124.5 %while.23 = (s32[]{:T(128)}, f32[4,128,128]{2,1,0:T(8,128)S(1)}, s32[]{:T(128)}, bf16[128,4,128,128]{3,2,1,0:T(8,128)(2,1)}, s32[]{:T(128)}, /*index=5*/s32[]{:T(128)}, s32[]{:T(128)}, s32[]{:T(128)}) while((s32[]{:T(128)}, f32[4,128,128]{2,1,0:T(8,128)S(1)}, s32[]{:T(128)}, bf16[128,4,128,128]{3,2,1,0:T(8,128)(2,1)}, s32[]{:T(128)}, ...), condition=%wide.region_6.7_spmd, body=%wide.region_5.6_spmd.sunk | while | flops 131078 | bytes 655503 | solution.py:24
  590.7 1.1 convert_add_fusion.5
  715.2 2.0 convolution_add_fusion.3
  717.2 1.8 copy.58
  719.0 1.4 fusion.4
  720.5 2.0 convolution_add_fusion.1
  722.5 1.6 fusion
  724.2 1.6 subtract_convert_fusion
  725.8 15.0 %reduce-scatter.5.cloned.1.call-done = bf16[128,512]{1,0:T(8,128)(2,1)} async-done(((bf16[128,2048]{1,0:T(8,128)(2,1)}), bf16[128,512]{1,0:T(8,128)(2,1)}) %reduce-scatter.5.cloned.1.call-update) | async-done | bytes 131088 | tf_op jit(solution)/shard_map/reduce_scatter | solution.py:127
  740.8 1.6 add_convert_fusion
  (181 shorter events, 131.8 us)
Async XLA Ops:
  7.2 92.8 %all-gather.13.cloned.1.call-start = ((), (), s32[]{:S(2)}) async-start(), calls=%async_computation.4 | async-start | bytes 2113536 | tf_op jit(solution)/shard_map/all_gather | solution.py:45
  7.9 175.0 %all-gather.9.cloned.1.call-start = ((), (), s32[]{:S(2)}) async-start(), calls=%async_computation.2 | async-start | bytes 2113536 | tf_op jit(solution)/shard_map/all_gather | solution.py:46
  8.6 257.2 %all-gather.11.cloned.1.call-start = ((), (), s32[]{:S(2)}) async-start(), calls=%async_computation.3 | async-start | bytes 2113536 | tf_op jit(solution)/shard_map/all_gather | solution.py:44
  9.4 357.5 %all-gather.17.cloned.1.call-start = ((), (), s32[]{:S(2)}) async-start(), calls=%async_computation.8 | async-start | bytes 16908288 | tf_op jit(solution)/shard_map/all_gather | solution.py:17
  102.7 166.0 %copy-start.3 = (bf16[128,512]{1,0:T(8,128)(2,1)}, bf16[128,512]{1,0:T(8,128)(2,1)S(1)}, u32[]{:S(2)}) copy-start(bf16[128,512]{1,0:T(8,128)(2,1)S(1)} %get-tuple-element.103) | copy-start | bytes 393220
  102.7 83.8 %copy-start.5 = (bf16[128,512]{1,0:T(8,128)(2,1)S(1)}, bf16[128,512]{1,0:T(8,128)(2,1)}, u32[]{:S(2)}) copy-start(bf16[128,512]{1,0:T(8,128)(2,1)} %param.15) | copy-start | bytes 393220
  185.8 265.0 %all-gather.15.cloned.1.call-start = ((), (), s32[]{:S(2)}) async-start(), calls=%async_computation.5 | async-start | bytes 2113536 | tf_op jit(solution)/shard_map/all_gather | solution.py:47
  186.4 404.3 %all-gather.19.cloned.1.call-start = ((), (), s32[]{:S(2)}) async-start(), calls=%async_computation.9 | async-start | bytes 16908288 | tf_op jit(solution)/shard_map/all_gather | solution.py:17
  366.9 83.9 %copy-start.8 = (f32[512]{0:T(512)S(1)}, f32[512]{0:T(512)}, u32[]{:S(2)}) copy-start(f32[512]{0:T(512)} %param.21) | copy-start | bytes 6148
  454.4 269.8 %reduce-scatter.3.cloned.1.call-start = ((), (), s32[]{:S(2)}) async-start(), calls=%async_computation.6 | async-start | bytes 655360 | tf_op jit(solution)/shard_map/reduce_scatter | solution.py:75
  456.0 5.2 copy-start
  457.8 3.4 copy-start.4
  461.1 279.6 %reduce-scatter.5.cloned.1.call-start = ((), (), s32[]{:S(2)}) async-start(), calls=%async_computation.7 | async-start | bytes 655360 | tf_op jit(solution)/shard_map/reduce_scatter | solution.py:127
  590.7 129.7 %copy-start.1 = (bf16[2048,512]{1,0:T(8,128)(2,1)S(1)}, bf16[2048,512]{1,0:T(8,128)(2,1)}, u32[]{:S(2)}) copy-start(bf16[2048,512]{1,0:T(8,128)(2,1)} %all-gather.13.cloned.1.call-done) | copy-start | bytes 6291460
  720.4 2.0 copy-start.2
  722.5 1.7 copy-start.6
  722.5 18.3 %copy-start.7 = (bf16[128,512]{1,0:T(8,128)(2,1)S(1)}, bf16[128,512]{1,0:T(8,128)(2,1)}, u32[]{:S(2)}) copy-start(bf16[128,512]{1,0:T(8,128)(2,1)} %param.16) | copy-start | bytes 393220
Sparse Core Ops, SparseCore 0:
  11.1 88.7 all-gather.12
  103.0 79.7 all-gather.8
  186.0 79.7 all-gather.10
  269.4 97.4 all-gather.16
  369.9 80.8 all-gather.14
  454.5 136.1 all-gather.18
  593.5 22.6 reduce-scatter.2
  724.3 16.4 reduce-scatter.4
where the time goes:
time: 753 us; the launch traced here: 749 us
  waiting for transfers between devices  553 us (73%)
  other arithmetic  126 us (17%)
  matrix products  27.3 us (4%)
  blocking collectives  22.3 us (3%)
  between operations  14.4 us (2%)
    all_gather x2, waiting for transfers between devices, prefix(): gathered = lax.all_gather(shard.astype(jnp.bfloat16), axis)  225 us
    add x127, other arithmetic, add_states(): return earlier + later  123 us
    all_gather x1, waiting for transfers between devices, per_device(): out_full = lax.all_gather(w_out, 'ctx', axis=1, tiled=True)  82.4 us
    all_gather x1, waiting for transfers between devices, per_device(): value_full = lax.all_gather(w_value, 'ctx', axis=0, tiled=True)  80.1 us
    all_gather x1, waiting for transfers between devices, per_device(): key_full = lax.all_gather(w_key, 'ctx', axis=0, tiled=True)  79.2 us
    all_gather x1, waiting for transfers between devices, per_device(): query_full = lax.all_gather(w_query, 'ctx', axis=0, tiled=True)  68.4 us
  transfers between devices with their start and end apart: 8, of which 7 were waited for; matrix products, arithmetic and copies ran while one was open for 20% of the time, Pallas kernels for 0%

commit v1 on v0

v1 whole, which is shorter than its diff:
```python
import jax
import jax.numpy as jnp
from jax import lax
from jax.experimental import pallas as pl
from jax.experimental.pallas import tpu as pltpu
from jax.sharding import PartitionSpec as P

MESH = pl.DeviceIdType.MESH
F32 = jnp.float32
BF16 = jnp.bfloat16
HEAD = 128
EPS = 1e-06
RING = 8
K, V, Q, O = 0, 1, 2, 3
FAR_FIRST = (4, 3, 5, 2, 6, 1, 7)


def dot_nn(a, b):
    return jnp.dot(a, b, preferred_element_type=F32)


def dot_nt(a, b):
    return lax.dot_general(a, b, (((1,), (1,)), ((), ())), preferred_element_type=F32)


def dot_tn(a, b):
    return lax.dot_general(a, b, (((0,), (0,)), ((), ())), preferred_element_type=F32)


def kernel(
    y_hbm, x_hbm, g_hbm, gs_hbm, wq_hbm, wk_hbm, wv_hbm, wo_hbm, gain_hbm,
    x_first, grad_x,
    wbuf, xg, y_v, gs_v, gain_v,
    q_v, k_v, v_v, slope_q, slope_k, gn_v, attn_s, back_v, dq_v, inner_v,
    st_src, st_in, st_pref, st_rs, st_row, st_po, st_p,
    own_v, core_out, core_in, hop_out, hop_in,
    loc_sem, wx_s, wx_r, p1_s, p1_r, p2_s, p2_r, xa_s, xa_r, xc_s, xc_r,
    st_s, st_r, rc_s, rc_r, rh_s, rh_r,
):
    ctx = lax.axis_index("ctx")
    x = lax.axis_index("tp")
    c = ctx % 2
    z = (ctx // 2) % RING
    y = ctx // (2 * RING)
    pending = []

    def at(yy, zz):
        return ((yy * RING + zz) * 2 + c, x)

    peer = (ctx + 1 - 2 * c, x)
    xr, xl, xo = (x + 1) % 4, (x + 3) % 4, (x + 2) % 4
    right, left = (ctx, xr), (ctx, xl)

    def remote(src, dst, ss, rs, dev):
        return pltpu.make_async_remote_copy(
            src_ref=src, dst_ref=dst, send_sem=ss, recv_sem=rs, device_id=dev, device_id_type=MESH
        )

    def send(src, dst, ss, rs, dev):
        copy = remote(src, dst, ss, rs, dev)
        copy.start()
        pending.append(copy)

    def arrive(dst, ss, rs):
        remote(dst, dst, ss, rs, peer).wait_recv()

    def drain():
        for copy in pending:
            copy.wait_send()
        pending.clear()

    mine = pl.ds(pl.multiple_of(c * 256, 256), 256)
    theirs = pl.ds(pl.multiple_of(256 - c * 256, 256), 256)
    shards = {K: wk_hbm, V: wv_hbm, Q: wq_hbm, O: wo_hbm}
    local = {}

    def stay(name, src, dst):
        local[name] = pltpu.make_async_copy(src, dst, loc_sem.at[len(local)])
        local[name].start()

    for w in (K, V, Q, O):
        stay(w, shards[w].at[:, mine], wbuf.at[w, y, z, c])
    stay("x", x_hbm, xg.at[0, x, 0])
    stay("g", g_hbm, xg.at[1, x, 0])
    stay("gain", gain_hbm, gain_v)
    stay("y", y_hbm, y_v)
    stay("gs", gs_hbm, gs_v)

    barrier = pltpu.get_barrier_semaphore()
    partners = [peer, right, left]
    partners += [at(y, (z + d) % RING) for d in range(1, RING)]
    partners += [at((y + d) % RING, z) for d in range(1, RING)]
    for dev in partners:
        pl.semaphore_signal(barrier, inc=1, device_id=dev, device_id_type=MESH)
    pl.semaphore_wait(barrier, len(partners))

    for w in (K, V, Q, O):
        send(shards[w].at[:, theirs], wbuf.at[w, y, z, c], wx_s.at[w], wx_r.at[w], peer)

    def gather_x(a, src):
        send(src, xg.at[a, x, 0], xa_s.at[a, 0], xa_r.at[a, 0], right)
        send(src, xg.at[a, x, 0], xa_s.at[a, 1], xa_r.at[a, 1], left)
        send(src, xg.at[a, x, 1], xc_s.at[a, 0], xc_r.at[a, 0], peer)

    lo, hi = pl.ds(0, 64), pl.ds(64, 64)

    def forward_x(a):
        arrive(xg.at[a, xl, 0], xa_s.at[a, 0], xa_r.at[a, 0])
        send(xg.at[a, xl, 0, lo], xg.at[a, xl, 0, lo], xa_s.at[a, 2], xa_r.at[a, 2], right)
        send(xg.at[a, xl, 0], xg.at[a, xl, 1], xc_s.at[a, 1], xc_r.at[a, 1], peer)
        arrive(xg.at[a, xr, 0], xa_s.at[a, 1], xa_r.at[a, 1])
        send(xg.at[a, xr, 0, hi], xg.at[a, xr, 0, hi], xa_s.at[a, 3], xa_r.at[a, 3], left)
        send(xg.at[a, xr, 0], xg.at[a, xr, 1], xc_s.at[a, 2], xc_r.at[a, 2], peer)

    def last_x(a):
        arrive(xg.at[a, xo, 0, lo], xa_s.at[a, 2], xa_r.at[a, 2])
        arrive(xg.at[a, xo, 0, hi], xa_s.at[a, 3], xa_r.at[a, 3])
        send(xg.at[a, xo, 0], xg.at[a, xo, 1], xc_s.at[a, 3], xc_r.at[a, 3], peer)

    def all_x(a):
        for i, src in enumerate((x, xl, xr, xo)):
            arrive(xg.at[a, src, 1], xc_s.at[a, i], xc_r.at[a, i])

    def along_y(w):
        return w in (V, O)

    def phase1(w):
        local[w].wait()
        arrive(wbuf.at[w, y, z, 1 - c], wx_s.at[w], wx_r.at[w])
        for d in FAR_FIRST:
            dev = at((y + d) % RING, z) if along_y(w) else at(y, (z + d) % RING)
            send(wbuf.at[w, y, z], wbuf.at[w, y, z], p1_s.at[w, d], p1_r.at[w, d], dev)

    def phase1_done(w):
        for d in FAR_FIRST:
            src = (RING - d) % RING
            dst = wbuf.at[w, (y + src) % RING, z] if along_y(w) else wbuf.at[w, y, (z + src) % RING]
            arrive(dst, p1_s.at[w, d], p1_r.at[w, d])

    def piece(w, index, half):
        part = pl.ds(half * 4, 4)
        return wbuf.at[w, part, index] if along_y(w) else wbuf.at[w, index, part]

    def ring(w, step):
        p = z if along_y(w) else y
        if along_y(w):
            ahead, behind = at(y, (z + 1) % RING), at(y, (z + 7) % RING)
        else:
            ahead, behind = at((y + 1) % RING, z), at((y + 7) % RING, z)
        for way, (dev, index) in enumerate(
            ((ahead, (p + RING - step) % RING), (behind, (p + step) % RING))
        ):
            for half in (0, 1) if way == 0 else (1, 0):
                block = piece(w, index, half)
                if step > 0 and not (step == 4 and half != way):
                    prev = (w, way, step - 1, half)
                    arrive(block, p2_s.at[prev], p2_r.at[prev])
                if step < 3 or (step == 3 and half == way):
                    this = (w, way, step, half)
                    send(block, block, p2_s.at[this], p2_r.at[this], dev)

    def state_out(turn, states):
        for h in range(2):
            st_src[turn, :, h] = states[h].astype(BF16).reshape(RING, 16, HEAD)
        st_in[turn, z] = st_src[turn, z]
        for d in FAR_FIRST:
            zt = (z + d) % RING
            send(st_src.at[turn, zt], st_in.at[turn, z], st_s.at[turn, 0, d], st_r.at[turn, 0, d], at(y, zt))

    def state_rows(turn):
        for d in FAR_FIRST:
            arrive(st_in.at[turn, (z + RING - d) % RING], st_s.at[turn, 0, d], st_r.at[turn, 0, d])
        total = jnp.zeros((2, 16, HEAD), F32)
        for i in range(RING) if turn == 0 else range(RING - 1, -1, -1):
            st_pref[i] = total
            total = total + st_in[turn, i].astype(F32)
        st_rs[turn] = total.astype(BF16)
        for d in FAR_FIRST:
            send(st_rs.at[turn], st_row.at[turn, y], st_s.at[turn, 1, d], st_r.at[turn, 1, d], at((y + d) % RING, z))
        st_row[turn, y] = st_rs[turn]

    def state_back(turn):
        for d in FAR_FIRST:
            arrive(st_row.at[turn, (y + RING - d) % RING], st_s.at[turn, 1, d], st_r.at[turn, 1, d])
        total = jnp.zeros((2, 16, HEAD), F32)
        for i in range(RING):
            use = (i < y) if turn == 0 else (i > y)
            total = total + jnp.where(use, st_row[turn, i].astype(F32), 0.0)
        for i in range(RING):
            st_po[turn, i] = (total + st_pref[i]).astype(BF16)
        st_p[turn, z] = st_po[turn, z]
        for d in FAR_FIRST:
            zt = (z + d) % RING
            send(st_po.at[turn, zt], st_p.at[turn, z], st_s.at[turn, 2, d], st_r.at[turn, 2, d], at(y, zt))

    def state_done(turn):
        for d in FAR_FIRST:
            arrive(st_p.at[turn, (z + RING - d) % RING], st_s.at[turn, 2, d], st_r.at[turn, 2, d])

    def state(turn, h):
        return st_p[turn, :, h].reshape(HEAD, HEAD)

    targets = {1: xr, 2: xo, 3: xl, 0: x}

    def rows_of(w, target):
        return wbuf[w, pl.ds(target * 2, 2)].reshape(512, 256)

    def sum_cores(a, product):
        for d in (2, 1, 3, 0):
            block = product(targets[d])
            core_out[a, d] = block[128:].astype(BF16)
            send(core_out.at[a, d], core_in.at[a, d], rc_s.at[a, d], rc_r.at[a, d], peer)
            own_v[d] = block[:128]

    def both(a, d):
        arrive(core_in.at[a, d], rc_s.at[a, d], rc_r.at[a, d])
        return own_v[d] + core_in[a, d].astype(F32)

    def hop(a, d, part, dev, i):
        send(hop_out.at[a, d, part], hop_in.at[a, d, part], rh_s.at[a, i], rh_r.at[a, i], dev)

    def landed(a, d, part, i):
        arrive(hop_in.at[a, d, part], rh_s.at[a, i], rh_r.at[a, i])

    def sum_first(a):
        hop_out[a, 2] = both(a, 2).astype(BF16)
        hop(a, 2, lo, right, 0)
        hop(a, 2, hi, left, 1)
        block = both(a, 1)
        hop_out[a, 1, 64:] = block[64:].astype(BF16)
        hop(a, 1, hi, right, 2)
        own_v[1] = block
        block = both(a, 3)
        hop_out[a, 3, :64] = block[:64].astype(BF16)
        hop(a, 3, lo, left, 3)
        own_v[3] = block

    def sum_second(a):
        landed(a, 2, lo, 0)
        hop_out[a, 1, :64] = (own_v[1, :64] + hop_in[a, 2, :64].astype(F32)).astype(BF16)
        hop(a, 1, lo, right, 4)
        landed(a, 2, hi, 1)
        hop_out[a, 3, 64:] = (own_v[3, 64:] + hop_in[a, 2, 64:].astype(F32)).astype(BF16)
        hop(a, 3, hi, left, 5)

    def sum_last(a):
        total = both(a, 0)
        landed(a, 1, hi, 2)
        landed(a, 3, lo, 3)
        landed(a, 1, lo, 4)
        landed(a, 3, hi, 5)
        return total + hop_in[a, 1].astype(F32) + hop_in[a, 3].astype(F32)

    def project(a, w):
        total = None
        for i in range(4):
            part = dot_nn(xg[a, i].reshape(256, 512), wbuf[w, 2 * i : 2 * i + 2].reshape(512, 256))
            total = part if total is None else total + part
        return total

    def feature(pre):
        return jnp.where(pre > 0, pre + 1.0, jnp.exp(jnp.minimum(pre, 0.0)))

    head = [slice(0, HEAD), slice(HEAD, 2 * HEAD)]
    place = [(lax.broadcasted_iota(jnp.int32, (256, 256), i) + c * 128) % 256 for i in range(2)]
    causal = place[0] >= place[1]

    phase1(K)
    phase1(V)
    gather_x(0, x_hbm)
    phase1_done(K)
    ring(K, 0)
    phase1_done(V)
    ring(V, 0)
    phase1(Q)
    phase1(O)
    ring(K, 1)
    ring(V, 1)
    forward_x(0)
    gather_x(1, g_hbm)
    ring(K, 2)
    ring(V, 2)
    last_x(0)
    phase1_done(Q)
    phase1_done(O)
    ring(K, 3)
    ring(V, 3)
    ring(Q, 0)
    ring(O, 0)
    forward_x(1)
    local["x"].wait()
    all_x(0)
    ring(K, 4)
    feat = feature(project(0, K))
    slope_k[...] = jnp.minimum(feat, 1.0)
    k_v[...] = feat.astype(BF16)
    ring(V, 4)
    v_v[...] = project(0, V).astype(BF16)
    state_out(0, [dot_tn(k_v[:, s], v_v[:, s]) for s in head])
    last_x(1)
    ring(Q, 1)
    ring(O, 1)
    state_rows(0)
    ring(Q, 2)
    ring(O, 2)
    state_back(0)
    ring(Q, 3)
    ring(O, 3)
    drain()
    local["g"].wait()
    local["gain"].wait()
    all_x(1)
    ring(Q, 4)
    feat = feature(project(0, Q))
    slope_q[...] = jnp.minimum(feat, 1.0)
    q_v[...] = feat.astype(BF16)
    for h, s in enumerate(head):
        scores = jnp.where(causal, dot_nt(q_v[:, s], k_v[:, s]), 0.0).astype(BF16)
        attn_s[h] = scores
        inner_v[:, s] = dot_nn(scores, v_v[:, s])
    ring(O, 4)
    gain = jnp.where(c == 0, gain_v[:, :256], gain_v[:, 256:])
    gn_v[...] = project(1, O) * gain

    state_done(0)
    normed = []
    backs = []
    for h, s in enumerate(head):
        attn = inner_v[:, s] + dot_nn(q_v[:, s], state(0, h))
        scale = lax.rsqrt(jnp.mean(attn * attn, axis=-1, keepdims=True) + EPS)
        unit = attn * scale
        normed.append((unit * gain[:, s]).astype(BF16))
        scaled = gn_v[:, s]
        back = ((scaled - unit * jnp.mean(unit * scaled, axis=-1, keepdims=True)) * scale).astype(BF16)
        back_v[:, s] = back
        backs.append(dot_tn(q_v[:, s], back))
    state_out(1, backs)
    normed = jnp.concatenate(normed, axis=1)
    sum_cores(0, lambda target: dot_nt(normed, rows_of(O, target)))
    sum_first(0)
    state_rows(1)
    for h, s in enumerate(head):
        back = back_v[:, s]
        gs = jnp.where(causal, dot_nt(back, v_v[:, s]), 0.0).astype(BF16)
        gq = dot_nn(gs, k_v[:, s]) + dot_nt(back, state(0, h))
        dq_v[0, :, s] = (gq * slope_q[:, s]).astype(BF16)
        gn_v[:, s] = dot_tn(gs, q_v[:, s])
        inner_v[:, s] = dot_tn(attn_s[h], back)
    state_back(1)
    sum_second(0)
    local["y"].wait()
    x_first[...] = (y_v[...].astype(F32) - sum_last(0)).astype(BF16)
    drain()

    state_done(1)
    for h, s in enumerate(head):
        later = state(1, h)
        gk = gn_v[:, s] + dot_nt(v_v[:, s], later)
        dq_v[1, :, s] = (gk * slope_k[:, s]).astype(BF16)
        dq_v[2, :, s] = (inner_v[:, s] + dot_nn(k_v[:, s], later)).astype(BF16)
    sum_cores(
        1,
        lambda target: dot_nt(dq_v[0], rows_of(Q, target))
        + dot_nt(dq_v[1], rows_of(K, target))
        + dot_nt(dq_v[2], rows_of(V, target)),
    )
    sum_first(1)
    sum_second(1)
    local["gs"].wait()
    grad_x[...] = (gs_v[...].astype(F32) + sum_last(1)).astype(BF16)
    drain()


def per_device(
    y_first, x_second, grad_first, grad_second, w_query, w_key, w_value, w_out, norm_gain
):
    dma = pltpu.SemaphoreType.DMA
    vm = pltpu.VMEM
    scratch = [
        vm((4, 8, 8, 2, 16, 256), BF16),
        vm((2, 4, 2, 128, 512), BF16),
        vm((128, 512), BF16),
        vm((128, 512), BF16),
        vm((1, 512), F32),
        vm((256, 256), BF16),
        vm((256, 256), BF16),
        vm((256, 256), BF16),
        vm((256, 256), F32),
        vm((256, 256), F32),
        vm((256, 256), F32),
        vm((2, 256, 256), BF16),
        vm((256, 256), BF16),
        vm((3, 256, 256), BF16),
        vm((256, 256), F32),
        vm((2, 8, 2, 16, 128), BF16),
        vm((2, 8, 2, 16, 128), BF16),
        vm((8, 2, 16, 128), F32),
        vm((2, 2, 16, 128), BF16),
        vm((2, 8, 2, 16, 128), BF16),
        vm((2, 8, 2, 16, 128), BF16),
        vm((2, 8, 2, 16, 128), BF16),
        vm((4, 128, 512), F32),
        vm((2, 4, 128, 512), BF16),
        vm((2, 4, 128, 512), BF16),
        vm((2, 4, 128, 512), BF16),
        vm((2, 4, 128, 512), BF16),
        dma((9,)),
        dma((4,)), dma((4,)),
        dma((4, 8)), dma((4, 8)),
        dma((4, 2, 4, 2)), dma((4, 2, 4, 2)),
        dma((2, 4)), dma((2, 4)),
        dma((2, 4)), dma((2, 4)),
        dma((2, 3, 8)), dma((2, 3, 8)),
        dma((2, 4)), dma((2, 4)),
        dma((2, 6)), dma((2, 6)),
    ]
    out = jax.ShapeDtypeStruct((128, 512), BF16)
    anywhere = pl.BlockSpec(memory_space=pl.ANY)
    return pl.pallas_call(
        kernel,
        out_shape=(out, out),
        in_specs=[anywhere] * 9,
        out_specs=(pl.BlockSpec(memory_space=pltpu.VMEM),) * 2,
        scratch_shapes=scratch,
        compiler_params=pltpu.CompilerParams(
            collective_id=0, has_side_effects=True, vmem_limit_bytes=48 * 2**20
        ),
        cost_estimate=pl.CostEstimate(
            flops=4_000_000_000, bytes_accessed=10_000_000, transcendentals=200_000
        ),
    )(
        y_first, x_second, grad_first, grad_second,
        w_query, w_key, w_value, w_out.T, norm_gain.reshape(1, 512),
    )


def solution(mesh):
    in_specs = (P("ctx", "tp"),) * 7 + (P("tp", "ctx"), P("tp"))
    out_specs = (P("ctx", "tp"), P("ctx", "tp"))
    return jax.shard_map(
        per_device, mesh=mesh, in_specs=in_specs, out_specs=out_specs, check_vma=False
    )
```

time: 753 us -> 95.2 us (0.13)
  waiting for transfers between devices: 553 us -> 0 us
  other arithmetic: 126 us -> 0 us
  Pallas kernels: 0 us -> 85.2 us
  matrix products: 27.3 us -> 0 us
  blocking collectives: 22.3 us -> 0 us
  between operations: 14.4 us -> 0.66 us
    all_gather x6 -> x0, waiting for transfers between devices: 536 us -> none  [the longest x2 225 us: prefix(): gathered = lax.all_gather(shard.astype(jnp.bfloat16), axis)]
    add x127 -> x0, other arithmetic: 123 us -> none  [add_states(): return earlier + later]
    pallas_call x0 -> x1, Pallas kernels: none -> 85.2 us  [per_device(): pl.pallas_call(kernel, out_shape=(out, out), in_specs=[anywhere] * 9, out...]
    dot_general x20 -> x0, matrix products: 27.3 us -> none  [the longest x1 3.32 us: per_device(): partial_out = jnp.dot(normed, out_full, preferred_element_type=jnp.float32)]
    all_gather x2 -> x0, blocking collectives: 22.3 us -> none  [the longest x1 11.3 us: per_device(): x_full = lax.all_gather(x_second, 'tp', axis=1, tiled=True)]
    reduce_scatter x2 -> x0, waiting for transfers between devices: 15 us -> none  [the longest x1 15 us: per_device(): lax.psum_scatter(terms.astype(jnp.bfloat16), 'tp', scatter_dimension=1, t...]
    unnamed x18 -> x20, local copies, waits for them, and re-layouts: 0.04 us -> 8.47 us
  transfers between devices with their start and end apart: 8 -> 0, of which waited for: 7 -> 0; matrix products, arithmetic and copies ran while one was open for 20% -> 0% of each run, Pallas kernels for 0% -> 0%
where the time goes in v1:
time: 95.2 us; the launch traced here: 94.4 us
  Pallas kernels  85.2 us (89%)
  local copies, waits for them, and re-layouts  8.47 us (9%)
    pallas_call x1, Pallas kernels, per_device(): pl.pallas_call(kernel, out_shape=(out, out), in_specs=[anywhere] * 9, out...  85.2 us
    unnamed x20, local copies, waits for them, and re-layouts  8.47 us

profile of v1, /device:TPU:1, one launch (start us, length us, event | category | flops | bytes accessed | tf_op | source)
XLA Modules:
  0.0 94.4 jit_solution(10692786160954055796)
XLA Ops:
  0.6 0.0 copy-start.8
  0.6 0.7 copy-done.8
  1.3 0.0 copy-start
  1.3 0.9 copy-done
  2.2 0.0 copy-start.1
  2.2 0.9 copy-done.1
  3.1 0.0 copy-start.2
  3.1 0.9 copy-done.2
  4.0 0.0 copy-start.3
  4.0 0.9 copy-done.3
  4.9 0.0 copy-start.4
  4.9 0.7 copy-done.4
  5.7 0.0 copy-start.5
  5.7 0.7 copy-done.5
  6.4 0.0 copy-start.6
  6.4 0.7 copy-done.6
  7.1 0.0 copy-start.7
  7.1 0.7 copy-done.7
  7.8 85.2 %shard_map.104 = (bf16[128,512]{1,0:T(8,128)(2,1)S(1)}, bf16[128,512]{1,0:T(8,128)(2,1)S(1)}) custom-call(bf16[128,512]{1,0:T(8,128)(2,1)S(1)} %copy-done, bf16[128,512]{1,0:T(8,128)(2,1)S(1)} %copy-done.1, bf16[128,512]{1,0:T(8,128)(2,1)S(1)} %copy-done.2, bf16[128,512]{1,0:T(8,128)(2,1)S(1)} %copy-done.3, bf16[16,512]{1,0:T(8,128)(2,1)S(1)} %copy-done.4, ...), custom_call_target="tpu_custom_call" | custom-call | flops 4000000000 | bytes 10000000 | tf_op jit(solution)/shard_map/pallas_call | solution.py:419
  93.1 0.7 copy.13
  93.7 0.7 copy.14
Async XLA Ops:
  0.6 0.7 copy-start.8
  1.3 0.9 copy-start
  2.2 0.9 copy-start.1
  3.1 0.9 copy-start.2
  4.0 0.9 copy-start.3
  4.9 0.7 copy-start.4
  5.7 0.7 copy-start.5
  6.4 0.7 copy-start.6
  7.1 0.7 copy-start.7

commit v2 on v1

v2 whole, which is shorter than its diff:
```python
import jax
import jax.numpy as jnp
from jax import lax
from jax.experimental import pallas as pl
from jax.experimental.pallas import tpu as pltpu
from jax.sharding import PartitionSpec as P

MESH = pl.DeviceIdType.MESH
F32 = jnp.float32
BF16 = jnp.bfloat16
HEAD = 128
EPS = 1e-06
RING = 8
K, V, Q, O = 0, 1, 2, 3
FAR_FIRST = (4, 3, 5, 2, 6, 1, 7)

S_SWAP, S_FIRST, S_SECOND, S_X, S_XC, S_STATE, S_CORE, S_HOP = 0, 1, 5, 9, 11, 13, 19, 21
SENT = 23
R_SWAP, R_FIRST, R_SECOND, R_X, R_XC, R_STATE, R_CORE, R_HOP = 0, 4, 36, 148, 160, 162, 168, 176
ARRIVED = 188


def dot_nn(a, b):
    return jnp.dot(a, b, preferred_element_type=F32)


def dot_nt(a, b):
    return lax.dot_general(a, b, (((1,), (1,)), ((), ())), preferred_element_type=F32)


def dot_tn(a, b):
    return lax.dot_general(a, b, (((0,), (0,)), ((), ())), preferred_element_type=F32)


def kernel(
    y_hbm, x_hbm, g_hbm, gs_hbm, wq_hbm, wk_hbm, wv_hbm, wo_hbm, gain_hbm,
    x_first, grad_x,
    wbuf, xg, y_v, gs_v, gain_v,
    q_v, k_v, v_v, slope_q, slope_k, gn_v, attn_s, back_v, normed_v, dq_v, inner_v,
    st_src, st_in, st_pref, st_rs, st_row, st_po, st_p, state_v, early_v,
    own_v, core_out, core_in, hop_out, hop_in,
    loc_sem, sent, arrived,
):
    ctx = lax.axis_index("ctx")
    x = lax.axis_index("tp")
    c = ctx % 2
    z = (ctx // 2) % RING
    y = ctx // (2 * RING)

    def at(yy, zz):
        return ((yy * RING + zz) * 2 + c, x)

    peer = (ctx + 1 - 2 * c, x)
    xr, xl, xo = (x + 1) % 4, (x + 3) % 4, (x + 2) % 4
    right, left = (ctx, xr), (ctx, xl)

    def remote(src, dst, ss, rs, dev):
        return pltpu.make_async_remote_copy(
            src_ref=src, dst_ref=dst, send_sem=ss, recv_sem=rs, device_id=dev, device_id_type=MESH
        )

    def send(src, dst, ss, rs, dev):
        remote(src, dst, ss, rs, dev).start()

    def arrive(dst, rs):
        remote(dst, dst, sent.at[0], rs, peer).wait_recv()

    def left_here(src, ss):
        remote(src, src, ss, arrived.at[0], peer).wait_send()

    mine = pl.ds(pl.multiple_of(c * 256, 256), 256)
    theirs = pl.ds(pl.multiple_of(256 - c * 256, 256), 256)
    shards = {K: wk_hbm, V: wv_hbm, Q: wq_hbm, O: wo_hbm}
    local = {}

    def stay(name, src, dst):
        local[name] = pltpu.make_async_copy(src, dst, loc_sem.at[len(local)])
        local[name].start()

    for w in (K, V, Q, O):
        stay(w, shards[w].at[:, mine], wbuf.at[w, y, z, c])
    stay("x", x_hbm, xg.at[0, x, 0])
    stay("g", g_hbm, xg.at[1, x, 0])
    stay("gain", gain_hbm, gain_v)
    stay("y", y_hbm, y_v)
    stay("gs", gs_hbm, gs_v)

    barrier = pltpu.get_barrier_semaphore()
    partners = [peer, right, left]
    partners += [at(y, (z + d) % RING) for d in range(1, RING)]
    partners += [at((y + d) % RING, z) for d in range(1, RING)]
    for dev in partners:
        pl.semaphore_signal(barrier, inc=1, device_id=dev, device_id_type=MESH)
    pl.semaphore_wait(barrier, len(partners))

    lo, hi = pl.ds(0, 64), pl.ds(64, 64)

    def x_hop(a, i, src, owner, part, dev):
        send(src.at[part], xg.at[a, owner, 0, part], sent.at[S_X + a], arrived.at[R_X + 6 * a + i], dev)

    def x_share(a, src, owner):
        send(src, xg.at[a, owner, 1], sent.at[S_XC + a], arrived.at[R_XC + a], peer)

    def x_here(a, i, owner, part):
        arrive(xg.at[a, owner, 0, part], arrived.at[R_X + 6 * a + i])

    def gather_x(a, src):
        x_hop(a, 0, src, x, lo, right)
        x_hop(a, 1, src, x, hi, left)
        x_hop(a, 2, src, x, hi, right)
        x_hop(a, 3, src, x, lo, left)
        x_share(a, src, x)

    def forward_x(a):
        x_here(a, 0, xl, lo)
        x_hop(a, 4, xg.at[a, xl, 0], xl, lo, right)
        x_here(a, 1, xr, hi)
        x_hop(a, 5, xg.at[a, xr, 0], xr, hi, left)

    def share_x(a):
        x_here(a, 2, xl, hi)
        x_share(a, xg.at[a, xl, 0], xl)
        x_here(a, 3, xr, lo)
        x_share(a, xg.at[a, xr, 0], xr)

    def last_x(a):
        x_here(a, 4, xo, lo)
        x_here(a, 5, xo, hi)
        x_share(a, xg.at[a, xo, 0], xo)

    def all_x(a):
        arrive(xg.at[a, :, 1], arrived.at[R_XC + a])

    def x_sent(a):
        left_here(xg.at[a, pl.ds(0, 3), 0], sent.at[S_X + a])
        left_here(xg.at[a, :, 1], sent.at[S_XC + a])

    def along_y(w):
        return w in (V, O)

    def first(w, shift):
        return at((y + shift) % RING, z) if along_y(w) else at(y, (z + shift) % RING)

    def second(w, shift):
        return at(y, (z + shift) % RING) if along_y(w) else at((y + shift) % RING, z)

    def block(w, one, two):
        if along_y(w):
            return wbuf.at[w, (y + one) % RING, (z + two) % RING]
        return wbuf.at[w, (y + two) % RING, (z + one) % RING]

    def shard_ready(w):
        local[w].wait()
        arrive(wbuf.at[w, y, z, 1 - c], arrived.at[R_SWAP + w])

    def spread(w):
        shard_ready(w)
        for d in FAR_FIRST:
            send(block(w, 0, 0), block(w, 0, 0), sent.at[S_FIRST + w], arrived.at[R_FIRST + 8 * w], first(w, d))

    def spread_done(w):
        arrive(wbuf.at[w, 0, pl.ds(0, 7)], arrived.at[R_FIRST + 8 * w])

    def ring_first(w, step):
        if step == 0:
            shard_ready(w)
        for way, sign in enumerate((-1, 1)):
            ref = block(w, (sign * step) % RING, 0)
            sem = R_FIRST + 8 * w + 4 * way + step
            if step > 0:
                arrive(ref.at[way] if step == 4 else ref, arrived.at[sem - 1])
            if step < 4:
                out = ref.at[way] if step == 3 else ref
                send(out, out, sent.at[S_FIRST + w], arrived.at[sem], first(w, -sign))

    def chunk(w, part, two):
        part = pl.ds(2 * part, 2)
        if along_y(w):
            return wbuf.at[w, part, (z + two) % RING]
        return wbuf.at[w, (y + two) % RING, part]

    def ring_second(w, step, i):
        for way, sign in enumerate((-1, 1)):
            ref = chunk(w, 3 - i if way else i, (sign * step) % RING)
            sem = R_SECOND + (w * 2 + way) * 14 + 4 * step + i
            if step > 0 and not (step == 4 and i > 1):
                arrive(ref, arrived.at[sem - 4])
            if step < 3 or (step == 3 and i < 2):
                send(ref, ref, sent.at[S_SECOND + w], arrived.at[sem], second(w, -sign))

    def weight_sent(w):
        left_here(wbuf.at[w, 0, pl.ds(0, 7)], sent.at[S_FIRST + w])
        left_here(wbuf.at[w, pl.ds(0, 7)], sent.at[S_SECOND + w])

    def exchange(turn, stage, src, dst, dev):
        index = 3 * turn + stage
        for d in FAR_FIRST:
            send(src(d), dst.at[turn, d], sent.at[S_STATE + index], arrived.at[R_STATE + index], dev(d))

    def exchanged(turn, stage, dst):
        arrive(dst.at[turn, pl.ds(1, 7)], arrived.at[R_STATE + 3 * turn + stage])

    def state_out(turn, states):
        for h in range(2):
            st_src[turn, :, h] = states[h].astype(BF16).reshape(RING, 16, HEAD)
        exchange(turn, 0, lambda d: st_src.at[turn, (z + d) % RING], st_in, lambda d: at(y, (z + d) % RING))
        st_in[turn, 0] = st_src[turn, z]

    def state_rows(turn):
        exchanged(turn, 0, st_in)
        total = jnp.zeros((2, 16, HEAD), F32)
        parts = []
        for i in range(RING) if turn == 0 else range(RING - 1, -1, -1):
            parts.append((i, total))
            total = total + st_in[turn, (z + RING - i) % RING].astype(F32)
        st_rs[turn] = total.astype(BF16)
        exchange(turn, 1, lambda d: st_rs.at[turn], st_row, lambda d: at((y + d) % RING, z))
        for i, part in parts:
            st_pref[i] = part

    def state_back(turn):
        exchanged(turn, 1, st_row)
        total = jnp.zeros((2, 16, HEAD), F32)
        for d in range(1, RING):
            use = (y >= d) if turn == 0 else (y < d)
            total = total + jnp.where(use, st_row[turn, d].astype(F32), 0.0)
        for i in range(RING):
            st_po[turn, i] = (total + st_pref[i]).astype(BF16)
        exchange(turn, 2, lambda d: st_po.at[turn, (z + d) % RING], st_p, lambda d: at(y, (z + d) % RING))
        st_p[turn, 0] = st_po[turn, z]

    def state_done(turn):
        exchanged(turn, 2, st_p)
        for j in range(RING):
            part = st_p[turn, (z + RING - j) % RING]
            for h in range(2):
                state_v[turn, h, pl.ds(16 * j, 16)] = part[h]

    def state(turn, h):
        return state_v[turn, h]

    def state_sent(turn):
        for stage in range(3):
            left_here(st_p.at[turn, pl.ds(1, 7)], sent.at[S_STATE + 3 * turn + stage])

    targets = {1: xr, 2: xo, 3: xl, 0: x}

    def rows_of(w, target):
        return wbuf[w, pl.ds(target * 2, 2)].reshape(512, 256)

    def sum_cores(a, product):
        for d in (2, 1, 3, 0):
            piece = product(d)
            core_out[a, d] = piece[128:].astype(BF16)
            send(core_out.at[a, d], core_in.at[a, d], sent.at[S_CORE + a], arrived.at[R_CORE + 4 * a + d], peer)
            own_v[d] = piece[:128]

    def both(a, d):
        arrive(core_in.at[a, d], arrived.at[R_CORE + 4 * a + d])
        return own_v[d] + core_in[a, d].astype(F32)

    def hop(a, d, part, dev, i):
        send(hop_out.at[a, d, part], hop_in.at[a, d, part], sent.at[S_HOP + a], arrived.at[R_HOP + 6 * a + i], dev)

    def landed(a, d, part, i):
        arrive(hop_in.at[a, d, part], arrived.at[R_HOP + 6 * a + i])

    def sum_first(a):
        hop_out[a, 2] = both(a, 2).astype(BF16)
        hop(a, 2, lo, right, 0)
        hop(a, 2, hi, left, 1)
        block = both(a, 1)
        hop_out[a, 1, 64:] = block[64:].astype(BF16)
        hop(a, 1, hi, right, 2)
        own_v[1] = block
        block = both(a, 3)
        hop_out[a, 3, :64] = block[:64].astype(BF16)
        hop(a, 3, lo, left, 3)
        own_v[3] = block

    def sum_second(a):
        landed(a, 2, lo, 0)
        hop_out[a, 1, :64] = (own_v[1, :64] + hop_in[a, 2, :64].astype(F32)).astype(BF16)
        hop(a, 1, lo, right, 4)
        landed(a, 2, hi, 1)
        hop_out[a, 3, 64:] = (own_v[3, 64:] + hop_in[a, 2, 64:].astype(F32)).astype(BF16)
        hop(a, 3, hi, left, 5)

    def sum_last(a):
        total = both(a, 0)
        landed(a, 1, hi, 2)
        landed(a, 3, lo, 3)
        landed(a, 1, lo, 4)
        landed(a, 3, hi, 5)
        return total + hop_in[a, 1].astype(F32) + hop_in[a, 3].astype(F32)

    def sums_sent(a):
        left_here(core_out.at[a], sent.at[S_CORE + a])
        left_here(hop_out.at[a, pl.ds(1, 3)], sent.at[S_HOP + a])

    def project(a, w):
        total = None
        for i in range(4):
            part = dot_nn(xg[a, i].reshape(256, 512), wbuf[w, 2 * i : 2 * i + 2].reshape(512, 256))
            total = part if total is None else total + part
        return total

    def feature(pre):
        return jnp.where(pre > 0, pre + 1.0, jnp.exp(jnp.minimum(pre, 0.0)))

    head = [slice(0, HEAD), slice(HEAD, 2 * HEAD)]
    place = [(lax.broadcasted_iota(jnp.int32, (256, 256), i) + c * 128) % 256 for i in range(2)]
    causal = place[0] >= place[1]

    for w in (K, V, Q, O):
        send(shards[w].at[:, theirs], wbuf.at[w, y, z, c], sent.at[S_SWAP], arrived.at[R_SWAP + w], peer)

    gather_x(0, x_hbm)
    spread(K)
    spread(V)
    gather_x(1, g_hbm)

    def serve(pair, step, pieces=range(4)):
        for i in pieces:
            for w in pair:
                ring_second(w, step, i)

    def serve_first(step):
        for w in (Q, O):
            ring_first(w, step)

    spread_done(K)
    spread_done(V)
    serve((K, V), 0)
    serve_first(0)
    forward_x(0)
    serve((K, V), 1)
    serve_first(1)
    share_x(0)
    serve((K, V), 2)
    serve_first(2)
    last_x(0)
    serve((K, V), 3)
    serve_first(3)
    serve_first(4)
    serve((Q, O), 0)
    local["x"].wait()
    all_x(0)
    serve((K, V), 4)
    feat = feature(project(0, K))
    slope_k[...] = jnp.minimum(feat, 1.0)
    k_v[...] = feat.astype(BF16)
    v_v[...] = project(0, V).astype(BF16)
    state_out(0, [dot_tn(k_v[:, s], v_v[:, s]) for s in head])
    serve((Q, O), 1)
    forward_x(1)
    share_x(1)
    state_rows(0)
    serve((Q, O), 2)
    last_x(1)
    state_back(0)
    serve((Q, O), 3)
    local["g"].wait()
    local["gain"].wait()
    all_x(1)
    serve((Q, O), 4)
    feat = feature(project(0, Q))
    slope_q[...] = jnp.minimum(feat, 1.0)
    q_v[...] = feat.astype(BF16)
    gain = jnp.where(c == 0, gain_v[:, :256], gain_v[:, 256:])
    gn_v[...] = project(1, O) * gain
    for h, s in enumerate(head):
        scores = jnp.where(causal, dot_nt(q_v[:, s], k_v[:, s]), 0.0).astype(BF16)
        attn_s[h] = scores
        inner_v[:, s] = dot_nn(scores, v_v[:, s])

    state_done(0)
    backs = []
    for h, s in enumerate(head):
        attn = inner_v[:, s] + dot_nn(q_v[:, s], state(0, h))
        scale = lax.rsqrt(jnp.mean(attn * attn, axis=-1, keepdims=True) + EPS)
        unit = attn * scale
        scaled = gn_v[:, s]
        back = ((scaled - unit * jnp.mean(unit * scaled, axis=-1, keepdims=True)) * scale).astype(BF16)
        back_v[:, s] = back
        backs.append(dot_tn(q_v[:, s], back))
        normed_v[:, s] = (unit * gain[:, s]).astype(BF16)
    state_out(1, backs)
    normed = normed_v[...]
    sum_cores(0, lambda d: dot_nt(normed, rows_of(O, targets[d])))
    sum_first(0)
    state_rows(1)
    for h, s in enumerate(head):
        back = back_v[:, s]
        gs = jnp.where(causal, dot_nt(back, v_v[:, s]), 0.0).astype(BF16)
        gq = dot_nn(gs, k_v[:, s]) + dot_nt(back, state(0, h))
        dq_v[0, :, s] = (gq * slope_q[:, s]).astype(BF16)
        gn_v[:, s] = dot_tn(gs, q_v[:, s])
        inner_v[:, s] = dot_tn(attn_s[h], back)
    state_back(1)
    sum_second(0)
    for d in range(4):
        early_v[d] = dot_nt(dq_v[0], rows_of(Q, targets[d]))
    local["y"].wait()
    x_first[...] = (y_v[...].astype(F32) - sum_last(0)).astype(BF16)
    left_here(wbuf.at[0, 0, pl.ds(0, 4), 0], sent.at[S_SWAP])
    for w in (K, V, Q, O):
        weight_sent(w)
    x_sent(0)
    x_sent(1)
    state_sent(0)
    sums_sent(0)

    state_done(1)
    for h, s in enumerate(head):
        later = state(1, h)
        gk = gn_v[:, s] + dot_nt(v_v[:, s], later)
        dq_v[1, :, s] = (gk * slope_k[:, s]).astype(BF16)
        dq_v[2, :, s] = (inner_v[:, s] + dot_nn(k_v[:, s], later)).astype(BF16)
    sum_cores(
        1,
        lambda d: early_v[d]
        + dot_nt(dq_v[1], rows_of(K, targets[d]))
        + dot_nt(dq_v[2], rows_of(V, targets[d])),
    )
    sum_first(1)
    sum_second(1)
    local["gs"].wait()
    grad_x[...] = (gs_v[...].astype(F32) + sum_last(1)).astype(BF16)
    state_sent(1)
    sums_sent(1)


def per_device(
    y_first, x_second, grad_first, grad_second, w_query, w_key, w_value, w_out, norm_gain
):
    dma = pltpu.SemaphoreType.DMA
    vm = pltpu.VMEM
    scratch = [
        vm((4, 8, 8, 2, 16, 256), BF16),
        vm((2, 4, 2, 128, 512), BF16),
        vm((128, 512), BF16),
        vm((128, 512), BF16),
        vm((1, 512), F32),
        vm((256, 256), BF16),
        vm((256, 256), BF16),
        vm((256, 256), BF16),
        vm((256, 256), F32),
        vm((256, 256), F32),
        vm((256, 256), F32),
        vm((2, 256, 256), BF16),
        vm((256, 256), BF16),
        vm((256, 256), BF16),
        vm((3, 256, 256), BF16),
        vm((256, 256), F32),
        vm((2, 8, 2, 16, 128), BF16),
        vm((2, 8, 2, 16, 128), BF16),
        vm((8, 2, 16, 128), F32),
        vm((2, 2, 16, 128), BF16),
        vm((2, 8, 2, 16, 128), BF16),
        vm((2, 8, 2, 16, 128), BF16),
        vm((2, 8, 2, 16, 128), BF16),
        vm((2, 2, 128, 128), BF16),
        vm((4, 256, 512), F32),
        vm((4, 128, 512), F32),
        vm((2, 4, 128, 512), BF16),
        vm((2, 4, 128, 512), BF16),
        vm((2, 4, 128, 512), BF16),
        vm((2, 4, 128, 512), BF16),
        dma((9,)),
        dma((SENT,)),
        dma((ARRIVED,)),
    ]
    out = jax.ShapeDtypeStruct((128, 512), BF16)
    anywhere = pl.BlockSpec(memory_space=pl.ANY)
    return pl.pallas_call(
        kernel,
        out_shape=(out, out),
        in_specs=[anywhere] * 9,
        out_specs=(pl.BlockSpec(memory_space=pltpu.VMEM),) * 2,
        scratch_shapes=scratch,
        compiler_params=pltpu.CompilerParams(
            collective_id=0, has_side_effects=True, vmem_limit_bytes=63_400_000
        ),
        cost_estimate=pl.CostEstimate(
            flops=4_000_000_000, bytes_accessed=10_000_000, transcendentals=200_000
        ),
    )(
        y_first, x_second, grad_first, grad_second,
        w_query, w_key, w_value, w_out.T, norm_gain.reshape(1, 512),
    )


def solution(mesh):
    in_specs = (P("ctx", "tp"),) * 7 + (P("tp", "ctx"), P("tp"))
    out_specs = (P("ctx", "tp"), P("ctx", "tp"))
    return jax.shard_map(
        per_device, mesh=mesh, in_specs=in_specs, out_specs=out_specs, check_vma=False
    )
```

time: 95.2 us -> 84.9 us (0.89)
  local copies, waits for them, and re-layouts: 8.47 us -> 2.26 us
  Pallas kernels: 85.2 us -> 81.8 us
    unnamed x20 -> x4, local copies, waits for them, and re-layouts: 8.47 us -> 2.26 us
    pallas_call x1, Pallas kernels: 85.2 us -> 81.8 us  [per_device(): pl.pallas_call(kernel, out_shape=(out, out), in_specs=[anywhere] * 9, out...]
where the time goes in v2:
time: 84.9 us; the launch traced here: 84.7 us
  Pallas kernels  81.8 us (96%)
  local copies, waits for them, and re-layouts  2.26 us (3%)
    pallas_call x1, Pallas kernels, per_device(): pl.pallas_call(kernel, out_shape=(out, out), in_specs=[anywhere] * 9, out...  81.8 us
    unnamed x4, local copies, waits for them, and re-layouts  2.26 us

profile of v2, /device:TPU:1, one launch (start us, length us, event | category | flops | bytes accessed | tf_op | source)
XLA Modules:
  0.0 84.7 jit_solution(9892389732276367935)
XLA Ops:
  0.6 81.8 %shard_map.104 = (bf16[128,512]{1,0:T(8,128)(2,1)}, bf16[128,512]{1,0:T(8,128)(2,1)}) custom-call(bf16[128,512]{1,0:T(8,128)(2,1)} %y_hbm.1, bf16[128,512]{1,0:T(8,128)(2,1)} %x_hbm.1, bf16[128,512]{1,0:T(8,128)(2,1)} %g_hbm.1, bf16[128,512]{1,0:T(8,128)(2,1)} %gs_hbm.1, bf16[16,512]{1,0:T(8,128)(2,1)} %wq_hbm.1, bf16[16,512]{1,0:T(8,128)(2,1)} %wk_hbm.1, ...), custom_call_target="tpu_custom_call" | custom-call | flops 4000000000 | bytes 10000000 | tf_op jit(solution)/shard_map/pallas_call | solution.py:476
  82.5 0.0 copy-start
  82.5 1.6 %copy.13 = bf16[128,512]{1,0:T(8,128)(2,1)} copy(bf16[128,512]{1,0:T(8,128)(2,1)} %get-tuple-element.4) | data formatting | bytes 262144
  84.1 0.0 copy-done
  84.1 0.7 copy.14
Async XLA Ops:
  82.5 1.6 %copy-start = (bf16[128,512]{1,0:T(8,128)(2,1)S(1)}, bf16[128,512]{1,0:T(8,128)(2,1)}, u32[]{:S(2)}) copy-start(bf16[128,512]{1,0:T(8,128)(2,1)} %get-tuple-element.5) | copy-start | bytes 393220

commit v3 on v2

--- a/solution.py
+++ b/solution.py
@@ -16,8 +16,10 @@
 
 S_SWAP, S_FIRST, S_SECOND, S_X, S_XC, S_STATE, S_CORE, S_HOP = 0, 1, 5, 9, 11, 13, 19, 21
 SENT = 23
-R_SWAP, R_FIRST, R_SECOND, R_X, R_XC, R_STATE, R_CORE, R_HOP = 0, 4, 36, 148, 160, 162, 168, 176
-ARRIVED = 188
+CHUNKS = (4, 4, 2, 2)
+R_SECOND = (22, 50, 78, 92)
+R_SWAP, R_FIRST, R_X, R_XC, R_STATE, R_CORE, R_HOP = 0, 4, 106, 118, 120, 126, 134
+ARRIVED = 146
 
 
 def dot_nn(a, b):
@@ -35,7 +37,7 @@
 def kernel(
     y_hbm, x_hbm, g_hbm, gs_hbm, wq_hbm, wk_hbm, wv_hbm, wo_hbm, gain_hbm,
     x_first, grad_x,
-    wbuf, xg, y_v, gs_v, gain_v,
+    wbuf, theirs_v, xg, y_v, gs_v, gain_v,
     q_v, k_v, v_v, slope_q, slope_k, gn_v, attn_s, back_v, normed_v, dq_v, inner_v,
     st_src, st_in, st_pref, st_rs, st_row, st_po, st_p, state_v, early_v,
     own_v, core_out, core_in, hop_out, hop_in,
@@ -50,7 +52,10 @@
     def at(yy, zz):
         return ((yy * RING + zz) * 2 + c, x)
 
-    peer = (ctx + 1 - 2 * c, x)
+    def across(dev):
+        return (dev[0] + 1 - 2 * c, x)
+
+    peer = across((ctx, x))
     xr, xl, xo = (x + 1) % 4, (x + 3) % 4, (x + 2) % 4
     right, left = (ctx, xr), (ctx, xl)
 
@@ -68,6 +73,14 @@
     def left_here(src, ss):
         remote(src, src, ss, arrived.at[0], peer).wait_send()
 
+    barrier = pltpu.get_barrier_semaphore()
+    partners = [peer, right, left]
+    partners += [at(y, (z + d) % RING) for d in range(1, RING)]
+    partners += [at((y + d) % RING, z) for d in range(1, RING)]
+    partners += [across(dev) for dev in partners[3:]]
+    for dev in partners:
+        pl.semaphore_signal(barrier, inc=1, device_id=dev, device_id_type=MESH)
+
     mine = pl.ds(pl.multiple_of(c * 256, 256), 256)
     theirs = pl.ds(pl.multiple_of(256 - c * 256, 256), 256)
     shards = {K: wk_hbm, V: wv_hbm, Q: wq_hbm, O: wo_hbm}
@@ -79,19 +92,14 @@
 
     for w in (K, V, Q, O):
         stay(w, shards[w].at[:, mine], wbuf.at[w, y, z, c])
+    for w in (K, V):
+        stay((w, "theirs"), shards[w].at[:, theirs], theirs_v.at[w])
     stay("x", x_hbm, xg.at[0, x, 0])
     stay("g", g_hbm, xg.at[1, x, 0])
     stay("gain", gain_hbm, gain_v)
     stay("y", y_hbm, y_v)
     stay("gs", gs_hbm, gs_v)
 
-    barrier = pltpu.get_barrier_semaphore()
-    partners = [peer, right, left]
-    partners += [at(y, (z + d) % RING) for d in range(1, RING)]
-    partners += [at((y + d) % RING, z) for d in range(1, RING)]
-    for dev in partners:
-        pl.semaphore_signal(barrier, inc=1, device_id=dev, device_id_type=MESH)
-    pl.semaphore_wait(barrier, len(partners))
 
     lo, hi = pl.ds(0, 64), pl.ds(64, 64)
 
@@ -154,19 +162,24 @@
         arrive(wbuf.at[w, y, z, 1 - c], arrived.at[R_SWAP + w])
 
     def spread(w):
-        shard_ready(w)
+        local[w].wait()
+        local[w, "theirs"].wait()
+        ref = wbuf.at[w, y, z, c]
         for d in FAR_FIRST:
-            send(block(w, 0, 0), block(w, 0, 0), sent.at[S_FIRST + w], arrived.at[R_FIRST + 8 * w], first(w, d))
+            send(ref, ref, sent.at[S_FIRST + w], arrived.at[R_FIRST + w], first(w, d))
+            send(theirs_v.at[w], ref, sent.at[S_FIRST + w], arrived.at[R_FIRST + w], across(first(w, d)))
+        swap(w, theirs_v.at[w])
 
     def spread_done(w):
-        arrive(wbuf.at[w, 0, pl.ds(0, 7)], arrived.at[R_FIRST + 8 * w])
+        arrive(wbuf.at[w, y, z, 1 - c], arrived.at[R_SWAP + w])
+        arrive(wbuf.at[w, 0, pl.ds(0, 7)], arrived.at[R_FIRST + w])
 
     def ring_first(w, step):
         if step == 0:
             shard_ready(w)
         for way, sign in enumerate((-1, 1)):
             ref = block(w, (sign * step) % RING, 0)
-            sem = R_FIRST + 8 * w + 4 * way + step
+            sem = R_FIRST + 2 + 8 * (w - Q) + 4 * way + step
             if step > 0:
                 arrive(ref.at[way] if step == 4 else ref, arrived.at[sem - 1])
             if step < 4:
@@ -174,18 +187,20 @@
                 send(out, out, sent.at[S_FIRST + w], arrived.at[sem], first(w, -sign))
 
     def chunk(w, part, two):
-        part = pl.ds(2 * part, 2)
+        size = 8 // CHUNKS[w]
+        part = pl.ds(size * part, size)
         if along_y(w):
             return wbuf.at[w, part, (z + two) % RING]
         return wbuf.at[w, (y + two) % RING, part]
 
     def ring_second(w, step, i):
+        count = CHUNKS[w]
         for way, sign in enumerate((-1, 1)):
-            ref = chunk(w, 3 - i if way else i, (sign * step) % RING)
-            sem = R_SECOND + (w * 2 + way) * 14 + 4 * step + i
-            if step > 0 and not (step == 4 and i > 1):
-                arrive(ref, arrived.at[sem - 4])
-            if step < 3 or (step == 3 and i < 2):
+            ref = chunk(w, count - 1 - i if way else i, (sign * step) % RING)
+            sem = R_SECOND[w] + way * 7 * count // 2 + count * step + i
+            if step > 0 and not (step == 4 and i >= count // 2):
+                arrive(ref, arrived.at[sem - count])
+            if step < 3 or (step == 3 and i < count // 2):
                 send(ref, ref, sent.at[S_SECOND + w], arrived.at[sem], second(w, -sign))
 
     def weight_sent(w):
@@ -312,16 +327,20 @@
     place = [(lax.broadcasted_iota(jnp.int32, (256, 256), i) + c * 128) % 256 for i in range(2)]
     causal = place[0] >= place[1]
 
-    for w in (K, V, Q, O):
-        send(shards[w].at[:, theirs], wbuf.at[w, y, z, c], sent.at[S_SWAP], arrived.at[R_SWAP + w], peer)
-
-    gather_x(0, x_hbm)
+    pl.semaphore_wait(barrier, len(partners))
+
+    def swap(w, src):
+        send(src, wbuf.at[w, y, z, c], sent.at[S_SWAP], arrived.at[R_SWAP + w], peer)
+
     spread(K)
     spread(V)
+    swap(Q, wq_hbm.at[:, theirs])
+    swap(O, wo_hbm.at[:, theirs])
+    gather_x(0, x_hbm)
     gather_x(1, g_hbm)
 
-    def serve(pair, step, pieces=range(4)):
-        for i in pieces:
+    def serve(pair, step):
+        for i in range(CHUNKS[pair[0]]):
             for w in pair:
                 ring_second(w, step, i)
 
@@ -438,6 +457,7 @@
     vm = pltpu.VMEM
     scratch = [
         vm((4, 8, 8, 2, 16, 256), BF16),
+        vm((2, 16, 256), BF16),
         vm((2, 4, 2, 128, 512), BF16),
         vm((128, 512), BF16),
         vm((128, 512), BF16),
@@ -467,7 +487,7 @@
         vm((2, 4, 128, 512), BF16),
         vm((2, 4, 128, 512), BF16),
         vm((2, 4, 128, 512), BF16),
-        dma((9,)),
+        dma((11,)),
         dma((SENT,)),
         dma((ARRIVED,)),
     ]

time: 84.9 us -> 84.2 us (level)
  no operation moved by 1% of the time
where the time goes in v3:
time: 84.2 us; the launch traced here: 84.1 us
  Pallas kernels  81.2 us (96%)
  local copies, waits for them, and re-layouts  2.26 us (3%)
    pallas_call x1, Pallas kernels, per_device(): pl.pallas_call(kernel, out_shape=(out, out), in_specs=[anywhere] * 9, out...  81.2 us
    unnamed x4, local copies, waits for them, and re-layouts  2.26 us

profile of v3, /device:TPU:1, one launch (start us, length us, event | category | flops | bytes accessed | tf_op | source)
XLA Modules:
  0.0 84.1 jit_solution(477033460227737494)
XLA Ops:
  0.6 81.2 %shard_map.104 = (bf16[128,512]{1,0:T(8,128)(2,1)}, bf16[128,512]{1,0:T(8,128)(2,1)}) custom-call(bf16[128,512]{1,0:T(8,128)(2,1)} %y_hbm.1, bf16[128,512]{1,0:T(8,128)(2,1)} %x_hbm.1, bf16[128,512]{1,0:T(8,128)(2,1)} %g_hbm.1, bf16[128,512]{1,0:T(8,128)(2,1)} %gs_hbm.1, bf16[16,512]{1,0:T(8,128)(2,1)} %wq_hbm.1, bf16[16,512]{1,0:T(8,128)(2,1)} %wk_hbm.1, ...), custom_call_target="tpu_custom_call" | custom-call | flops 4000000000 | bytes 10000000 | tf_op jit(solution)/shard_map/pallas_call | solution.py:496
  81.8 0.0 copy-start
  81.8 1.6 %copy.13 = bf16[128,512]{1,0:T(8,128)(2,1)} copy(bf16[128,512]{1,0:T(8,128)(2,1)} %get-tuple-element.4) | data formatting | bytes 262144
  83.4 0.0 copy-done
  83.4 0.7 copy.14
Async XLA Ops:
  81.8 1.6 %copy-start = (bf16[128,512]{1,0:T(8,128)(2,1)S(1)}, bf16[128,512]{1,0:T(8,128)(2,1)}, u32[]{:S(2)}) copy-start(bf16[128,512]{1,0:T(8,128)(2,1)} %get-tuple-element.5) | copy-start | bytes 393220

commit v4 on v3

--- a/solution.py
+++ b/solution.py
@@ -36,7 +36,7 @@
 
 def kernel(
     y_hbm, x_hbm, g_hbm, gs_hbm, wq_hbm, wk_hbm, wv_hbm, wo_hbm, gain_hbm,
-    x_first, grad_x,
+    results,
     wbuf, theirs_v, xg, y_v, gs_v, gain_v,
     q_v, k_v, v_v, slope_q, slope_k, gn_v, attn_s, back_v, normed_v, dq_v, inner_v,
     st_src, st_in, st_pref, st_rs, st_row, st_po, st_p, state_v, early_v,
@@ -421,7 +421,8 @@
     for d in range(4):
         early_v[d] = dot_nt(dq_v[0], rows_of(Q, targets[d]))
     local["y"].wait()
-    x_first[...] = (y_v[...].astype(F32) - sum_last(0)).astype(BF16)
+    y_v[...] = (y_v[...].astype(F32) - sum_last(0)).astype(BF16)
+    stay("first", y_v, results.at[0])
     left_here(wbuf.at[0, 0, pl.ds(0, 4), 0], sent.at[S_SWAP])
     for w in (K, V, Q, O):
         weight_sent(w)
@@ -445,9 +446,12 @@
     sum_first(1)
     sum_second(1)
     local["gs"].wait()
-    grad_x[...] = (gs_v[...].astype(F32) + sum_last(1)).astype(BF16)
+    gs_v[...] = (gs_v[...].astype(F32) + sum_last(1)).astype(BF16)
+    stay("second", gs_v, results.at[1])
     state_sent(1)
     sums_sent(1)
+    local["first"].wait()
+    local["second"].wait()
 
 
 def per_device(
@@ -487,17 +491,17 @@
         vm((2, 4, 128, 512), BF16),
         vm((2, 4, 128, 512), BF16),
         vm((2, 4, 128, 512), BF16),
-        dma((11,)),
+        dma((13,)),
         dma((SENT,)),
         dma((ARRIVED,)),
     ]
     out = jax.ShapeDtypeStruct((128, 512), BF16)
     anywhere = pl.BlockSpec(memory_space=pl.ANY)
-    return pl.pallas_call(
+    results = pl.pallas_call(
         kernel,
-        out_shape=(out, out),
+        out_shape=jax.ShapeDtypeStruct((2, 128, 512), BF16),
         in_specs=[anywhere] * 9,
-        out_specs=(pl.BlockSpec(memory_space=pltpu.VMEM),) * 2,
+        out_specs=anywhere,
         scratch_shapes=scratch,
         compiler_params=pltpu.CompilerParams(
             collective_id=0, has_side_effects=True, vmem_limit_bytes=63_400_000
@@ -509,6 +513,7 @@
         y_first, x_second, grad_first, grad_second,
         w_query, w_key, w_value, w_out.T, norm_gain.reshape(1, 512),
     )
+    return results[0], results[1]
 
 
 def solution(mesh):

time: 84.2 us -> 83.6 us (level)
    unnamed x4 -> x0, local copies, waits for them, and re-layouts: 2.26 us -> none
    squeeze x0 -> x1, local copies, waits for them, and re-layouts: none -> 1.68 us  [per_device(): return (results[0], results[1])]
where the time goes in v4:
time: 83.6 us; the launch traced here: 83.5 us
  Pallas kernels  81.2 us (97%)
  local copies, waits for them, and re-layouts  1.68 us (2%)
    pallas_call x1, Pallas kernels, per_device(): pl.pallas_call(kernel, out_shape=jax.ShapeDtypeStruct((2, 128, 512), BF16...  81.2 us
    squeeze x1, local copies, waits for them, and re-layouts, per_device(): return (results[0], results[1])  1.68 us

profile of v4, /device:TPU:1, one launch (start us, length us, event | category | flops | bytes accessed | tf_op | source)
XLA Modules:
  0.0 83.5 jit_solution(13311866852277108715)
XLA Ops:
  0.6 81.2 %shard_map.104 = bf16[2,128,512]{2,1,0:T(8,128)(2,1)} custom-call(bf16[128,512]{1,0:T(8,128)(2,1)} %y_hbm.1, bf16[128,512]{1,0:T(8,128)(2,1)} %x_hbm.1, bf16[128,512]{1,0:T(8,128)(2,1)} %g_hbm.1, bf16[128,512]{1,0:T(8,128)(2,1)} %gs_hbm.1, bf16[16,512]{1,0:T(8,128)(2,1)} %wq_hbm.1, bf16[16,512]{1,0:T(8,128)(2,1)} %wk_hbm.1, bf16[16,512]{1,0:T(8,128)(2,1)} %wv_hbm.1, ...), custom_call_target="tpu_custom_call" | custom-call | flops 4000000000 | bytes 10000000 | tf_op jit(solution)/shard_map/pallas_call | solution.py:500
  81.8 1.7 %slice_bitcast_fusion = (bf16[128,512]{1,0:T(8,128)(2,1)}, bf16[128,512]{1,0:T(8,128)(2,1)}) fusion(bf16[2,128,512]{2,1,0:T(8,128)(2,1)} %shard_map.104), kind=kLoop, calls=%fused_computation | loop fusion | bytes 524288 | tf_op jit(solution)/shard_map/squeeze | solution.py:516

commit v5 on v4

--- a/solution.py
+++ b/solution.py
@@ -74,10 +74,11 @@
         remote(src, src, ss, arrived.at[0], peer).wait_send()
 
     barrier = pltpu.get_barrier_semaphore()
-    partners = [peer, right, left]
-    partners += [at(y, (z + d) % RING) for d in range(1, RING)]
-    partners += [at((y + d) % RING, z) for d in range(1, RING)]
-    partners += [across(dev) for dev in partners[3:]]
+    partners = []
+    for d in FAR_FIRST:
+        for dev in (at(y, (z + d) % RING), at((y + d) % RING, z)):
+            partners += [dev, across(dev)]
+    partners += [right, left, peer]
     for dev in partners:
         pl.semaphore_signal(barrier, inc=1, device_id=dev, device_id_type=MESH)
 
@@ -161,14 +162,18 @@
         local[w].wait()
         arrive(wbuf.at[w, y, z, 1 - c], arrived.at[R_SWAP + w])
 
-    def spread(w):
-        local[w].wait()
-        local[w, "theirs"].wait()
-        ref = wbuf.at[w, y, z, c]
+    def spread(pair):
+        for w in pair:
+            local[w].wait()
+            local[w, "theirs"].wait()
         for d in FAR_FIRST:
-            send(ref, ref, sent.at[S_FIRST + w], arrived.at[R_FIRST + w], first(w, d))
-            send(theirs_v.at[w], ref, sent.at[S_FIRST + w], arrived.at[R_FIRST + w], across(first(w, d)))
-        swap(w, theirs_v.at[w])
+            for w in pair:
+                ref = wbuf.at[w, y, z, c]
+                sems = sent.at[S_FIRST + w], arrived.at[R_FIRST + w]
+                send(ref, ref, *sems, first(w, d))
+                send(theirs_v.at[w], ref, *sems, across(first(w, d)))
+        for w in pair:
+            swap(w, theirs_v.at[w])
 
     def spread_done(w):
         arrive(wbuf.at[w, y, z, 1 - c], arrived.at[R_SWAP + w])
@@ -332,8 +337,7 @@
     def swap(w, src):
         send(src, wbuf.at[w, y, z, c], sent.at[S_SWAP], arrived.at[R_SWAP + w], peer)
 
-    spread(K)
-    spread(V)
+    spread((K, V))
     swap(Q, wq_hbm.at[:, theirs])
     swap(O, wo_hbm.at[:, theirs])
     gather_x(0, x_hbm)
@@ -348,19 +352,19 @@
         for w in (Q, O):
             ring_first(w, step)
 
+    serve_first(0)
     spread_done(K)
     spread_done(V)
     serve((K, V), 0)
-    serve_first(0)
+    serve_first(1)
     forward_x(0)
     serve((K, V), 1)
-    serve_first(1)
+    serve_first(2)
     share_x(0)
     serve((K, V), 2)
-    serve_first(2)
+    serve_first(3)
     last_x(0)
     serve((K, V), 3)
-    serve_first(3)
     serve_first(4)
     serve((Q, O), 0)
     local["x"].wait()

time: 83.6 us -> 80.4 us (0.962)
  Pallas kernels: 81.2 us -> 77.9 us
    pallas_call x1, Pallas kernels: 81.2 us -> 77.9 us  [per_device(): pl.pallas_call(kernel, out_shape=jax.ShapeDtypeStruct((2, 128, 512), BF16...]
where the time goes in v5:
time: 80.4 us; the launch traced here: 80.2 us
  Pallas kernels  77.9 us (97%)
  local copies, waits for them, and re-layouts  1.68 us (2%)
    pallas_call x1, Pallas kernels, per_device(): pl.pallas_call(kernel, out_shape=jax.ShapeDtypeStruct((2, 128, 512), BF16...  77.9 us
    squeeze x1, local copies, waits for them, and re-layouts, per_device(): return (results[0], results[1])  1.68 us

profile of v5, /device:TPU:1, one launch (start us, length us, event | category | flops | bytes accessed | tf_op | source)
XLA Modules:
  0.0 80.2 jit_solution(4990416536497644995)
XLA Ops:
  0.6 77.9 %shard_map.104 = bf16[2,128,512]{2,1,0:T(8,128)(2,1)} custom-call(bf16[128,512]{1,0:T(8,128)(2,1)} %y_hbm.1, bf16[128,512]{1,0:T(8,128)(2,1)} %x_hbm.1, bf16[128,512]{1,0:T(8,128)(2,1)} %g_hbm.1, bf16[128,512]{1,0:T(8,128)(2,1)} %gs_hbm.1, bf16[16,512]{1,0:T(8,128)(2,1)} %wq_hbm.1, bf16[16,512]{1,0:T(8,128)(2,1)} %wk_hbm.1, bf16[16,512]{1,0:T(8,128)(2,1)} %wv_hbm.1, ...), custom_call_target="tpu_custom_call" | custom-call | flops 4000000000 | bytes 10000000 | tf_op jit(solution)/shard_map/pallas_call | solution.py:504
  78.6 1.7 %slice_bitcast_fusion = (bf16[128,512]{1,0:T(8,128)(2,1)}, bf16[128,512]{1,0:T(8,128)(2,1)}) fusion(bf16[2,128,512]{2,1,0:T(8,128)(2,1)} %shard_map.104), kind=kLoop, calls=%fused_computation | loop fusion | bytes 524288 | tf_op jit(solution)/shard_map/squeeze | solution.py:520

commit v6 on v5

--- a/solution.py
+++ b/solution.py
@@ -366,10 +366,10 @@
     last_x(0)
     serve((K, V), 3)
     serve_first(4)
-    serve((Q, O), 0)
     local["x"].wait()
     all_x(0)
     serve((K, V), 4)
+    serve((Q, O), 0)
     feat = feature(project(0, K))
     slope_k[...] = jnp.minimum(feat, 1.0)
     k_v[...] = feat.astype(BF16)

time: 80.4 us -> 81.9 us (1.019)
  Pallas kernels: 77.9 us -> 79.4 us
    pallas_call x1, Pallas kernels: 77.9 us -> 79.4 us  [per_device(): pl.pallas_call(kernel, out_shape=jax.ShapeDtypeStruct((2, 128, 512), BF16...]
where the time goes in v6:
time: 81.9 us; the launch traced here: 81.7 us
  Pallas kernels  79.4 us (97%)
  local copies, waits for them, and re-layouts  1.68 us (2%)
    pallas_call x1, Pallas kernels, per_device(): pl.pallas_call(kernel, out_shape=jax.ShapeDtypeStruct((2, 128, 512), BF16...  79.4 us
    squeeze x1, local copies, waits for them, and re-layouts, per_device(): return (results[0], results[1])  1.68 us

profile of v6, /device:TPU:1, one launch (start us, length us, event | category | flops | bytes accessed | tf_op | source)
XLA Modules:
  0.0 81.7 jit_solution(13040709385426828955)
XLA Ops:
  0.6 79.4 %shard_map.104 = bf16[2,128,512]{2,1,0:T(8,128)(2,1)} custom-call(bf16[128,512]{1,0:T(8,128)(2,1)} %y_hbm.1, bf16[128,512]{1,0:T(8,128)(2,1)} %x_hbm.1, bf16[128,512]{1,0:T(8,128)(2,1)} %g_hbm.1, bf16[128,512]{1,0:T(8,128)(2,1)} %gs_hbm.1, bf16[16,512]{1,0:T(8,128)(2,1)} %wq_hbm.1, bf16[16,512]{1,0:T(8,128)(2,1)} %wk_hbm.1, bf16[16,512]{1,0:T(8,128)(2,1)} %wv_hbm.1, ...), custom_call_target="tpu_custom_call" | custom-call | flops 4000000000 | bytes 10000000 | tf_op jit(solution)/shard_map/pallas_call | solution.py:504
  80.0 1.7 %slice_bitcast_fusion = (bf16[128,512]{1,0:T(8,128)(2,1)}, bf16[128,512]{1,0:T(8,128)(2,1)}) fusion(bf16[2,128,512]{2,1,0:T(8,128)(2,1)} %shard_map.104), kind=kLoop, calls=%fused_computation | loop fusion | bytes 524288 | tf_op jit(solution)/shard_map/squeeze | solution.py:520
